TPU v7x, 256 devices: a whole 4x4x8 slice. The times are simulated.
256 devices in a mesh: row: 16 (over y, x), col: 16 (over z, core).
Axes of the slice: x: 4, y: 4, z: 8, core: 2. Of those that a mesh axis runs over, the one named last changes fastest.
Arguments:
- matrix: float32 [20480, 20480], P('row', 'col'), as said below
Outputs:
- factored: float32 [20480, 20480], P('row', 'col')
Inputs may be any that keep to these rules, and one draw needn't show every extreme that they name: `matrix`: symmetric positive definite in global order, stored in the tile storage of the statement.
All inputs are finite; a program needn't handle non-finite values.
Results may differ from a plain program's by a relative error of at most 0.000053.
Values sent between devices are 32-bit elements; how exact they have to be, the bound alone decides.
A program may use at most 128 MiB of HBM per device.

v0:
```python
import jax
import jax.numpy as jnp
from jax import lax
from jax.sharding import PartitionSpec as P

TILE = 128


def spread(block, axis, source):
    block = jnp.where(lax.axis_index(axis) == source, block, jnp.zeros_like(block))
    return lax.psum(block, axis)


def product_t(left, right):
    return lax.dot_general(
        left,
        right,
        (((1,), (1,)), ((), ())),
        precision=lax.Precision.HIGHEST,
        preferred_element_type=jnp.float32,
    )


def column_of(work, panel, tile, col_count):
    start = panel // col_count * tile
    return work[:, start : start + tile]


def gathered_columns(rows_panel, tile, row_count, row_tiles, col_global):
    whole = lax.all_gather(rows_panel, "row", axis=0, tiled=True)
    blocks = whole.reshape(row_count * row_tiles, tile, tile)
    tile_index = col_global % row_count * row_tiles + col_global // row_count
    return jnp.take(blocks, tile_index, axis=0).reshape(-1, tile)


def factor_panel(
    strip, panel, tile, row_count, col_count, row_tiles, row_global, col_global, col_here
):
    owner_row = panel % row_count
    local_row = panel // row_count
    corner = strip[local_row * tile : (local_row + 1) * tile]
    corner = spread(corner, "row", owner_row)
    lower = jnp.linalg.cholesky(corner)
    identity = jnp.eye(tile, dtype=lower.dtype)
    inverse = lax.linalg.triangular_solve(lower, identity, left_side=True, lower=True)
    solved = product_t(strip, inverse).reshape(row_tiles, tile, tile)
    below = (row_global > panel)[:, None, None]
    at_panel = (row_global == panel)[:, None, None]
    trail = jnp.where(below, solved, 0.0)
    written = jnp.where(at_panel, lower[None], trail).reshape(-1, tile)
    trail = trail.reshape(-1, tile)
    rows_panel = spread(trail, "col", panel % col_count)
    cols_panel = gathered_columns(rows_panel, tile, row_count, row_tiles, col_global)
    return (written, rows_panel, cols_panel)


def finish_panel(
    work, panel, written, tile, row_count, col_count, col_tiles, row_here, col_here, col_global
):
    start = panel // col_count * tile
    block = work[:, start : start + tile]
    work = work.at[:, start : start + tile].set(
        jnp.where(col_here == panel % col_count, written, block)
    )
    row_start = panel // row_count * tile
    band = work[row_start : row_start + tile].reshape(tile, col_tiles, tile)
    keep = jnp.logical_or(row_here != panel % row_count, col_global <= panel)[None, :, None]
    band = jnp.where(keep, band, 0.0).reshape(tile, -1)
    return work.at[row_start : row_start + tile].set(band)


def per_device(matrix):
    tile = TILE
    row_count = lax.axis_size("row")
    col_count = lax.axis_size("col")
    row_here = lax.axis_index("row")
    col_here = lax.axis_index("col")
    row_tiles = matrix.shape[0] // tile
    col_tiles = matrix.shape[1] // tile
    row_global = jnp.arange(row_tiles, dtype=jnp.int32) * row_count + row_here
    col_global = jnp.arange(col_tiles, dtype=jnp.int32) * col_count + col_here
    shared = (tile, row_count, col_count, row_tiles, row_global, col_global, col_here)
    work = matrix
    written_one, rows_one, cols_one = factor_panel(column_of(work, 0, tile, col_count), 0, *shared)
    work = work - product_t(rows_one, cols_one)
    work = finish_panel(
        work, 0, written_one, tile, row_count, col_count, col_tiles, row_here, col_here, col_global
    )
    written_two, rows_two, cols_two = factor_panel(column_of(work, 1, tile, col_count), 1, *shared)
    work = work - product_t(rows_two, cols_two)
    work = finish_panel(
        work, 1, written_two, tile, row_count, col_count, col_tiles, row_here, col_here, col_global
    )
    return work


def solution(mesh):
    in_specs = (P("row", "col"),)
    out_specs = P("row", "col")
    return jax.shard_map(
        per_device, mesh=mesh, in_specs=in_specs, out_specs=out_specs, check_vma=False
    )
```

profile of v0, /device:TPU:240, one launch (start us, length us, event | category | flops | bytes accessed | tf_op | source)
XLA Modules:
  0.0 726.5 jit_solution(5358653501307688207)
XLA Ops:
  6.5 0.0 all-reduce.5.cloned.1.call-start
  6.5 8.1 %copy.17 = f32[1280,1280]{0,1:T(8,128)} copy(f32[1280,1280]{1,0:T(8,128)} %param.14) | data formatting | bytes 13107200 | tf_op args[0]
  14.7 1.5 slice_select_fusion.3
  16.1 0.0 all-reduce.5.cloned.1.call-update
  16.1 0.0 all-reduce.7.cloned.1.call-start
  16.2 0.1 broadcast_bitcast_fusion.5
  16.3 90.3 %all-reduce.5.cloned.1.call-done = f32[128,128]{0,1:T(8,128)} async-done(((f32[128,128]{0,1:T(8,128)}), f32[128,128]{0,1:T(8,128)}) %all-reduce.5.cloned.1.call-update) | async-done | bytes 65552 | tf_op jit(solution)/shard_map/psum | solution.py:11
  106.6 0.9 copy.14
  107.5 0.9 fusion.13
  108.3 11.7 %cholesky.44 = f32[128,128]{1,0:T(8,128)S(1)} custom-call(f32[128,128]{1,0:T(8,128)S(1)} %fusion.13), custom_call_target="Cholesky" | custom-call | tf_op jit(solution)/shard_map/jit(cholesky)/cholesky | solution.py:43
  120.1 0.7 compare_reduce_fusion.1
  120.8 0.7 select_bitcast_fusion.1
  121.5 9.8 %custom-call.6 = f32[1,128,128]{1,2,0:T(8,128)S(1)} custom-call(f32[1,128,128]{2,1,0:T(8,128)S(1)} %get-tuple-element.60), custom_call_target="InvertDiagBlocksLowerTriangular" | custom-call | tf_op jit(solution)/shard_map/triangular_solve/custom-call.0 | solution.py:45
  131.3 0.3 fusion.8
  131.6 2.6 broadcast_select_fusion.3
  134.2 0.0 all-reduce.7.cloned.1.call-update
  134.3 0.0 all-gather.3.cloned.1.call-start
  134.3 107.6 %all-reduce.7.cloned.1.call-done = f32[1280,128]{0,1:T(8,128)} async-done(((f32[1280,128]{0,1:T(8,128)}), f32[1280,128]{0,1:T(8,128)}) %all-reduce.7.cloned.1.call-update) | async-done | bytes 655376 | tf_op jit(solution)/shard_map/psum | solution.py:11
  241.9 0.0 all-gather.3.cloned.1.call-update
  242.0 0.0 all-reduce.9.cloned.1.call-start
  242.0 0.7 compare_reduce_fusion.2
  242.8 0.1 broadcast_bitcast_fusion.4
  242.9 0.1 broadcast_bitcast_fusion.3
  243.0 0.2 copy.19
  243.3 0.0 copy-start
  243.3 90.0 %all-gather.3.cloned.1.call-done = f32[20480,128]{0,1:T(8,128)} async-done(((f32[1280,128]{0,1:T(8,128)}), f32[20480,128]{0,1:T(8,128)}) %all-gather.3.cloned.1.call-update) | async-done | bytes 10485776 | tf_op jit(solution)/shard_map/all_gather | solution.py:30
  333.3 11.7 %copy.29 = f32[20480,128]{1,0:T(8,128)} copy(f32[20480,128]{0,1:T(8,128)} %all-gather.3.cloned.1.call-done) | data formatting | bytes 20971520 | tf_op jit(solution)/shard_map/reshape | solution.py:31
  345.0 4.6 gather_fusion
  349.6 0.1 broadcast_select_fusion.1
  349.7 0.0 copy-done
  349.7 9.2 %convolution_subtract_fusion.1 = f32[1280,1280]{0,1:T(8,128)} fusion(f32[1280,1280]{0,1:T(8,128)} %copy.17, f32[1280,128]{0,1:T(8,128)S(1)} %copy-done, f32[1280,128]{1,0:T(8,128)S(1)} %bitcast.47), kind=kOutput, calls=%fused_computation.3 | convolution fusion | flops 2518220800 | bytes 14417920 | tf_op jit(solution)/shard_map/dot_general | solution.py:15
  358.9 2.7 fusion.1
  361.6 2.2 constant_dynamic-update-slice_fusion
  363.8 0.6 slice_select_fusion.2
  364.4 0.0 all-reduce.9.cloned.1.call-update
  364.4 0.2 all-reduce.11.cloned.1.call-start
  364.6 0.1 broadcast_bitcast_fusion.2
  364.7 89.7 %all-reduce.9.cloned.1.call-done = f32[128,128]{0,1:T(8,128)} async-done(((f32[128,128]{0,1:T(8,128)}), f32[128,128]{0,1:T(8,128)}) %all-reduce.9.cloned.1.call-update) | async-done | bytes 65552 | tf_op jit(solution)/shard_map/psum | solution.py:11
  454.4 0.9 copy.20
  455.3 0.9 fusion.11
  456.2 11.7 %cholesky.55 = f32[128,128]{1,0:T(8,128)S(1)} custom-call(f32[128,128]{1,0:T(8,128)S(1)} %fusion.11), custom_call_target="Cholesky" | custom-call | tf_op jit(solution)/shard_map/jit(cholesky)/cholesky | solution.py:43
  467.9 0.7 compare_reduce_fusion
  468.6 0.7 select_bitcast_fusion
  469.4 9.8 %custom-call.7 = f32[1,128,128]{1,2,0:T(8,128)S(1)} custom-call(f32[1,128,128]{2,1,0:T(8,128)S(1)} %get-tuple-element.56), custom_call_target="InvertDiagBlocksLowerTriangular" | custom-call | tf_op jit(solution)/shard_map/triangular_solve/custom-call.0 | solution.py:45
  479.2 0.3 fusion.6
  479.5 2.6 broadcast_select_fusion.2
  482.1 0.0 all-reduce.11.cloned.1.call-update
  482.1 0.0 all-gather.5.cloned.1.call-start
  482.2 107.6 %all-reduce.11.cloned.1.call-done = f32[1280,128]{0,1:T(8,128)} async-done(((f32[1280,128]{0,1:T(8,128)}), f32[1280,128]{0,1:T(8,128)}) %all-reduce.11.cloned.1.call-update) | async-done | bytes 655376 | tf_op jit(solution)/shard_map/psum | solution.py:11
  589.8 0.0 all-gather.5.cloned.1.call-update
  589.8 0.1 broadcast_bitcast_fusion.1
  589.9 0.1 broadcast_bitcast_fusion
  590.1 0.2 copy.24
  590.3 0.0 copy-start.1
  590.3 90.7 %all-gather.5.cloned.1.call-done = f32[20480,128]{0,1:T(8,128)} async-done(((f32[1280,128]{0,1:T(8,128)}), f32[20480,128]{0,1:T(8,128)}) %all-gather.5.cloned.1.call-update) | async-done | bytes 10485776 | tf_op jit(solution)/shard_map/all_gather | solution.py:30
  681.0 11.7 %copy.30 = f32[20480,128]{1,0:T(8,128)} copy(f32[20480,128]{0,1:T(8,128)} %all-gather.5.cloned.1.call-done) | data formatting | bytes 20971520 | tf_op jit(solution)/shard_map/reshape | solution.py:31
  692.7 4.6 gather_fusion.1
  697.3 0.1 broadcast_select_fusion
  697.4 0.0 copy-done.1
  697.4 9.2 %convolution_subtract_fusion = f32[1280,1280]{0,1:T(8,128)} fusion(f32[1280,1280]{0,1:T(8,128)} %get-tuple-element.58, f32[1280,128]{0,1:T(8,128)S(1)} %copy-done.1, f32[1280,128]{1,0:T(8,128)S(1)} %bitcast.46), kind=kOutput, calls=%fused_computation.2 | convolution fusion | flops 2518220800 | bytes 14417920 | tf_op jit(solution)/shard_map/dot_general | solution.py:15
  706.6 2.7 fusion.2
  709.3 2.3 fusion.3
  711.6 8.1 %copy.25 = f32[1280,1280]{1,0:T(8,128)} copy(f32[1280,1280]{0,1:T(8,128)} %fusion.3) | data formatting | bytes 13107200 | tf_op jit(solution)/shard_map/scatter | solution.py:69
  (12 shorter events, 0.3 us)
Async XLA Ops:
  6.5 100.0 %all-reduce.5.cloned.1.call-start = ((), (), s32[]{:S(2)}) async-start(), calls=%async_computation | async-start | bytes 131072 | tf_op jit(solution)/shard_map/psum | solution.py:11
  16.1 225.8 %all-reduce.7.cloned.1.call-start = ((), (), s32[]{:S(2)}) async-start(), calls=%async_computation.1 | async-start | bytes 1310720 | tf_op jit(solution)/shard_map/psum | solution.py:11
  134.3 199.0 %all-gather.3.cloned.1.call-start = ((), (), s32[]{:S(2)}) async-start(), calls=%async_computation.2 | async-start | bytes 11141120 | tf_op jit(solution)/shard_map/all_gather | solution.py:30
  242.0 212.4 %all-reduce.9.cloned.1.call-start = ((), (), s32[]{:S(2)}) async-start(), calls=%async_computation.3 | async-start | bytes 131072 | tf_op jit(solution)/shard_map/psum | solution.py:11
  243.3 106.5 %copy-start = (f32[1280,128]{0,1:T(8,128)S(1)}, f32[1280,128]{0,1:T(8,128)}, u32[]{:S(2)}) copy-start(f32[1280,128]{0,1:T(8,128)} %all-reduce.7.cloned.1.call-done) | copy-start | bytes 1966084
  364.4 225.4 %all-reduce.11.cloned.1.call-start = ((), (), s32[]{:S(2)}) async-start(), calls=%async_computation.4 | async-start | bytes 1310720 | tf_op jit(solution)/shard_map/psum | solution.py:11
  482.1 198.9 %all-gather.5.cloned.1.call-start = ((), (), s32[]{:S(2)}) async-start(), calls=%async_computation.5 | async-start | bytes 11141120 | tf_op jit(solution)/shard_map/all_gather | solution.py:30
  590.3 107.1 %copy-start.1 = (f32[1280,128]{0,1:T(8,128)S(1)}, f32[1280,128]{0,1:T(8,128)}, u32[]{:S(2)}) copy-start(f32[1280,128]{0,1:T(8,128)} %all-reduce.11.cloned.1.call-done) | copy-start | bytes 1966084
Sparse Core Ops, SparseCore 0:
  16.3 90.2 all-reduce.4
  134.4 107.4 all-reduce.6
  244.4 88.8 all-gather.2
  364.5 89.8 all-reduce.8
  482.2 107.4 all-reduce.10
  592.1 88.8 all-gather.4
where the time goes:
time: 732 us; the launch traced here: 727 us
  waiting for transfers between devices  576 us (79%)
  other arithmetic  60.6 us (8%)
  local copies, waits for them, and re-layouts  51.7 us (7%)
  matrix products  24.1 us (3%)
  between operations  13.7 us (2%)
    psum x4, waiting for transfers between devices, spread(): return lax.psum(block, axis)  395 us
    all_gather x2, waiting for transfers between devices, gathered_columns(): whole = lax.all_gather(rows_panel, 'row', axis=0, tiled=True)  181 us
    another operation x6, other arithmetic, factor_panel(): lower = jnp.linalg.cholesky(corner)  24.9 us
    dot_general x4, matrix products, product_t(): lax.dot_general(left, right, (((1,), (1,)), ((), ())), precision=lax.Prec...  23.6 us
    reshape x2, local copies, waits for them, and re-layouts, gathered_columns(): blocks = whole.reshape(row_count * row_tiles, tile, tile)  23.5 us
    another operation x4, other arithmetic, factor_panel(): lax.linalg.triangular_solve(lower, identity, left_side=True, lower=True)  21 us
  transfers between devices with their start and end apart: 6, of which 6 were waited for; matrix products, arithmetic and copies ran while one was open for 0% of the time, Pallas kernels for 0%

commit v1 on v0

v1 whole, which is shorter than its diff:
```python
import functools

import jax
import jax.numpy as jnp
from jax import lax
from jax.experimental import pallas as pl
from jax.experimental.pallas import tpu as pltpu
from jax.sharding import PartitionSpec as P

TILE = 128
SUP = 64
SIDE = 1280
RING_X = 4
RING_Y = 4
RING_Z = 8
ZCH = 20
ZROWS = SIDE // ZCH
PCH = 5
LAG = 2
EXACT = lax.Precision.HIGHEST
MESH = pl.DeviceIdType.MESH


def dot(left, right, dims):
    return lax.dot_general(
        left, right, (dims, ((), ())), precision=EXACT, preferred_element_type=jnp.float32
    )


def cholesky_inverse(tile):
    sub = lax.broadcasted_iota(jnp.int32, (8, TILE), 0)
    lane = lax.broadcasted_iota(jnp.int32, (8, TILE), 1)
    count = TILE // 8
    a = [tile[8 * i : 8 * i + 8] for i in range(count)]
    w = [jnp.where(lane == sub + 8 * i, 1.0, 0.0) for i in range(count)]
    for start in range(0, TILE, SUP):
        blocks = list(range(start // 8, (start + SUP) // 8))
        for t in blocks:
            j0 = 8 * t
            rest = [m for m in blocks if m >= t]
            col = {
                m: [jnp.broadcast_to(a[m][:, j0 + q : j0 + q + 1], (8, TILE)) for q in range(8)]
                for m in rest
            }
            scale = jnp.zeros((8, TILE), jnp.float32)
            for p in range(8):
                root = lax.rsqrt(jnp.broadcast_to(col[t][p][p : p + 1], (8, TILE)))
                scale = jnp.where(sub == p, root, scale)
                row_a = jnp.broadcast_to(a[t][p : p + 1], (8, TILE)) * root
                row_w = jnp.broadcast_to(w[t][p : p + 1], (8, TILE)) * root
                piece = {
                    q: jnp.broadcast_to(col[t][q][p : p + 1], (8, TILE)) * root
                    for q in range(p + 1, 8)
                }
                for m in rest:
                    factor = col[m][p] * root
                    for q in range(p + 1, 8):
                        col[m][q] = col[m][q] - factor * piece[q]
                    if m == t:
                        factor = jnp.where(sub > p, factor, 0.0)
                    a[m] = a[m] - factor * row_a
                    w[m] = w[m] - factor * row_w
            a[t] = jnp.where(lane >= sub + j0, a[t] * scale, 0.0)
            w[t] = w[t] * scale
        end = start + SUP
        if end < TILE:
            upper = jnp.concatenate([a[m] for m in blocks], 0)
            both = jnp.concatenate([upper, jnp.concatenate([w[m] for m in blocks], 0)], 1)
            change = dot(upper, both, ((0,), (0,)))
            for m in range(end // 8, count):
                a[m] = a[m] - change[8 * m : 8 * m + 8, :TILE]
                w[m] = w[m] - change[8 * m : 8 * m + 8, TILE:]
    return jnp.concatenate(a, 0), jnp.concatenate(w, 0)


def place():
    r = lax.axis_index("row")
    c = lax.axis_index("col")
    return r % RING_X, r // RING_X, c // 2, c % 2


def device(x, y, z, k):
    return (y * RING_X + x, z * 2 + k)


def wrap(i, n):
    return lax.rem(i + n, n)


def panels_kernel(
    a_ref, pr_ref, pc_hi_ref, pc_lo_ref, u_ref,
    hr, hc, cn, w_all,
    cn_recv, cn_send, cn_sib, z_recv, z_send, z_sib_recv, z_sib_send, z_own,
    p_recv, px_send, py_send, p_own,
):
    x, y, z, k = place()
    r = y * RING_X + x
    flat = r
    sibling = device(x, y, z, 1 - k)
    pos = jnp.where(k == 0, z, wrap(RING_Z - z, RING_Z))
    step = 1 - 2 * k
    z_next = device(x, y, wrap(z + step, RING_Z), k)

    barrier = pltpu.get_barrier_semaphore()

    def greet(target):
        pl.semaphore_signal(barrier, inc=1, device_id=target, device_id_type=MESH)

    greet(sibling)
    greet(device(x, y, wrap(z + 1, RING_Z), k))
    greet(device(x, y, wrap(z - 1, RING_Z), k))
    greet(device(wrap(x + 1, RING_X), y, z, k))
    greet(device(wrap(x - 1, RING_X), y, z, k))
    greet(device(x, wrap(y + 1, RING_Y), z, k))
    greet(device(x, wrap(y - 1, RING_Y), z, k))
    root_here = [
        jnp.logical_and(flat == 0, k == 0),
        jnp.logical_and(flat == 0, k == 1),
        jnp.logical_and(flat == 1, k == 1),
    ]
    root_row = (0, 0, 1)
    root_core = (0, 1, 1)
    count = jnp.int32(7)
    for tile in range(3):
        mine = k == root_core[tile]

        @pl.when(jnp.logical_and(mine, flat != root_row[tile]))
        def _(tile=tile):
            greet((root_row[tile], z * 2 + root_core[tile]))

        @pl.when(jnp.logical_and(root_here[tile], z != 0))
        def _(tile=tile):
            greet((root_row[tile], root_core[tile]))

        count = count + jnp.where(root_here[tile], 15 + jnp.where(z == 0, 7, 0), 0)
    pl.semaphore_wait(barrier, count)

    def remote(src, dst, send, recv, target):
        return pltpu.make_async_remote_copy(
            src_ref=src, dst_ref=dst, send_sem=send, recv_sem=recv, device_id=target,
            device_id_type=MESH,
        )

    corner_src = a_ref.at[0:TILE, 0:TILE]
    for tile in range(3):

        @pl.when(jnp.logical_and(root_here[tile], z == 0))
        def _(tile=tile):
            @pl.loop(1, RING_Z)
            def _(i):
                remote(
                    corner_src, cn.at[tile], cn_send.at[tile], cn_recv.at[tile],
                    (root_row[tile], i * 2 + root_core[tile]),
                ).start()

            own = pltpu.make_async_copy(corner_src, cn.at[tile], cn_recv.at[tile])
            own.start()

    for tile in range(3):

        @pl.when(k == root_core[tile])
        def _(tile=tile):
            pltpu.make_async_copy(corner_src, cn.at[tile], cn_recv.at[tile]).wait()

            @pl.when(root_here[tile])
            def _():
                @pl.loop(1, 16)
                def _(i):
                    remote(
                        cn.at[tile], cn.at[tile], cn_send.at[tile], cn_recv.at[tile],
                        (wrap(root_row[tile] + i, 16), z * 2 + root_core[tile]),
                    ).start()

            remote(cn.at[tile], cn.at[tile], cn_sib.at[tile], cn_recv.at[tile], sibling).start()

    def z_chunk(j):
        rows = pl.ds(pl.multiple_of(j * ZROWS, ZROWS), ZROWS)
        here = hr.at[k, rows]

        def send(src):
            @pl.when(pos < RING_Z - 1)
            def _():
                remote(src, here, z_send, z_recv.at[j], z_next).start()

            remote(src, here, z_sib_send, z_sib_recv, sibling).start()

        @pl.when(pos == 0)
        def _():
            send(a_ref.at[rows, 0:TILE])

        @pl.when(pos != 0)
        def _():
            pltpu.make_async_copy(here, here, z_recv.at[j]).wait()
            send(here)

    def p_chunk(s, d, j):
        sign = 1 - 2 * d
        lanes = slice((d * PCH + j) * TILE, (d * PCH + j + 1) * TILE)
        here = hc.at[s, :, lanes]
        index = (s * 2 + d) * PCH + j
        xpos = wrap((x - s) * sign + RING_X, RING_X)
        ypos = wrap(y * sign, RING_Y)
        source = flat == s
        go_x = jnp.logical_and(xpos < RING_X - 1, jnp.logical_or(k == 1, y == 0))
        go_y = jnp.logical_and(ypos < RING_Y - 1, jnp.logical_or(k == 0, x == s))

        def send(src):
            @pl.when(go_x)
            def _():
                remote(
                    src, here, px_send.at[index], p_recv.at[index],
                    device(wrap(x + sign, RING_X), y, z, k),
                ).start()

            @pl.when(go_y)
            def _():
                remote(
                    src, here, py_send.at[index], p_recv.at[index],
                    device(x, wrap(y + sign, RING_Y), z, k),
                ).start()

        @pl.when(source)
        def _():
            send(a_ref.at[0:TILE, lanes])

        @pl.when(jnp.logical_not(source))
        def _():
            pltpu.make_async_copy(here, here, p_recv.at[index]).wait()
            send(here)

    @pl.when(pos == 0)
    def _():
        pltpu.make_async_copy(a_ref.at[:, 0:TILE], hr.at[k], z_own).start()

    @pl.when(flat < 2)
    def _():
        pltpu.make_async_copy(a_ref.at[0:TILE, :], hc.at[flat], p_own).start()

    hops = {}
    for s in range(2):
        for d in range(2):
            sign = 1 - 2 * d
            hops[s, d] = wrap((x - s) * sign + RING_X, RING_X) + wrap(y * sign, RING_Y)

    slots = ZCH + LAG * (RING_Z - 1)
    for slot in range(slots):
        j = slot - LAG * pos

        @pl.when(jnp.logical_and(j >= 0, j < ZCH))
        def _(j=j):
            z_chunk(j)

        for s in range(2):
            for d in range(2):
                for jj in range(PCH):
                    at = slot - 4 * jj - 2 * s - d
                    if 0 <= at <= LAG * 6 and at % LAG == 0:

                        @pl.when(hops[s, d] == at // LAG)
                        def _(s=s, d=d, jj=jj):
                            p_chunk(s, d, jj)

    for tile in range(3):

        @pl.when(k != root_core[tile])
        def _(tile=tile):
            pltpu.make_async_copy(cn.at[tile], cn.at[tile], cn_recv.at[tile]).wait()

        @pl.when(k == root_core[tile])
        def _(tile=tile):
            remote(cn.at[tile], cn.at[tile], cn_sib.at[tile], cn_recv.at[tile], sibling).wait_send()

            def drain(n):
                @pl.loop(0, n)
                def _(i):
                    remote(
                        cn.at[tile], cn.at[tile], cn_send.at[tile], cn_recv.at[tile], sibling
                    ).wait_send()

            @pl.when(root_here[tile])
            def _():
                drain(15)

            @pl.when(jnp.logical_and(root_here[tile], z == 0))
            def _():
                drain(7)

    u0, w0 = cholesky_inverse(cn[0])
    u01 = dot(w0, cn[1], ((1,), (0,)))
    u1, w1 = cholesky_inverse(cn[2] - dot(u01, u01, ((0,), (0,))))
    w10 = -dot(w1, dot(u01, w0, ((0,), (0,))), ((1,), (0,)))
    w_all[:TILE, :TILE] = w0
    w_all[:TILE, TILE:] = jnp.zeros((TILE, TILE), jnp.float32)
    w_all[TILE:, :TILE] = w10
    w_all[TILE:, TILE:] = w1
    u_ref[0] = u0.T
    u_ref[1] = u1.T

    whole_r = hr.at[k]
    other_r = hr.at[1 - k]
    pltpu.make_async_copy(other_r, other_r, z_sib_recv).wait()

    @pl.when(pos == 0)
    def _():
        pltpu.make_async_copy(a_ref.at[:, 0:TILE], hr.at[k], z_own).wait()

    @pl.when(flat < 2)
    def _():
        pltpu.make_async_copy(a_ref.at[0:TILE, :], hc.at[flat], p_own).wait()

    @pl.loop(0, SIDE // 256)
    def _(i):
        rows = pl.ds(pl.multiple_of(i * 256, 256), 256)
        raw = jnp.concatenate([hr[0, rows], hr[1, rows]], axis=1)
        pr_ref[rows] = dot(raw, w_all[...], ((1,), (1,)))

    for i in range(SIDE // 256):
        lanes = slice(i * 256, i * 256 + 256)
        raw = jnp.concatenate([hc[0, :, lanes], hc[1, :, lanes]], axis=0)
        got = dot(w_all[...], raw, ((1,), (0,)))
        high = got.astype(jnp.bfloat16)
        pc_hi_ref[:, lanes] = high
        pc_lo_ref[:, lanes] = (got - high.astype(jnp.float32)).astype(jnp.bfloat16)

    remote(whole_r, whole_r, z_sib_send, z_sib_recv, sibling).wait_send()

    @pl.when(pos < RING_Z - 1)
    def _():
        remote(whole_r, whole_r, z_send, z_sib_recv, sibling).wait_send()

    for s in range(2):
        for d in range(2):
            sign = 1 - 2 * d
            xpos = wrap((x - s) * sign + RING_X, RING_X)
            ypos = wrap(y * sign, RING_Y)
            go_x = jnp.logical_and(xpos < RING_X - 1, jnp.logical_or(k == 1, y == 0))
            go_y = jnp.logical_and(ypos < RING_Y - 1, jnp.logical_or(k == 0, x == s))
            for jj in range(PCH):
                index = (s * 2 + d) * PCH + jj
                here = hc.at[s, :, (d * PCH + jj) * TILE : (d * PCH + jj + 1) * TILE]

                @pl.when(go_x)
                def _(here=here, index=index):
                    remote(here, here, px_send.at[index], p_recv.at[index], sibling).wait_send()

                @pl.when(go_y)
                def _(here=here, index=index):
                    remote(here, here, py_send.at[index], p_recv.at[index], sibling).wait_send()


def panels(matrix):
    vmem = pl.BlockSpec(memory_space=pltpu.VMEM)
    f32 = jnp.float32
    dma = pltpu.SemaphoreType.DMA
    return pl.pallas_call(
        panels_kernel,
        out_shape=[
            jax.ShapeDtypeStruct((SIDE, 2 * TILE), f32),
            jax.ShapeDtypeStruct((2 * TILE, SIDE), jnp.bfloat16),
            jax.ShapeDtypeStruct((2 * TILE, SIDE), jnp.bfloat16),
            jax.ShapeDtypeStruct((2, TILE, TILE), f32),
        ],
        in_specs=[pl.BlockSpec(memory_space=pl.ANY)],
        out_specs=[vmem] * 4,
        scratch_shapes=[
            pltpu.VMEM((2, SIDE, TILE), f32),
            pltpu.VMEM((2, TILE, SIDE), f32),
            pltpu.VMEM((3, TILE, TILE), f32),
            pltpu.VMEM((2 * TILE, 2 * TILE), f32),
            dma((3,)), dma((3,)), dma((3,)),
            dma((ZCH,)), dma, dma, dma, dma,
            dma((4 * PCH,)), dma((4 * PCH,)), dma((4 * PCH,)), dma,
        ],
        compiler_params=pltpu.CompilerParams(
            collective_id=0, has_side_effects=True, vmem_limit_bytes=40 * 2**20
        ),
        name="panels",
    )(matrix)


def update_kernel(a_ref, pr_ref, pc_hi_ref, pc_lo_ref, u_ref, out_ref):
    i = pl.program_id(0)
    r = lax.axis_index("row")
    c = lax.axis_index("col")
    high = pr_ref[...].astype(jnp.bfloat16)
    low = (pr_ref[...] - high.astype(jnp.float32)).astype(jnp.bfloat16)

    def part(left, right):
        return lax.dot_general(
            left, right[...], (((1,), (0,)), ((), ())), preferred_element_type=jnp.float32
        )

    out_ref[...] = a_ref[...] - (
        part(high, pc_hi_ref) + (part(high, pc_lo_ref) + part(low, pc_hi_ref))
    )

    @pl.when(c == 0)
    def _():
        out_ref[:, :TILE] = pr_ref[:, :TILE]

    @pl.when(c == 1)
    def _():
        out_ref[:, :TILE] = pr_ref[:, TILE:]

    @pl.when(jnp.logical_and(i == 0, r < 2))
    def _():
        @pl.when(jnp.logical_or(c != 0, r == 0))
        def _():
            out_ref[:TILE, :TILE] = jnp.where(c == r, u_ref[r], 0.0)

        out_ref[:TILE, TILE:] = jnp.zeros((TILE, SIDE - TILE), jnp.float32)


def update(matrix, pr, pc_hi, pc_lo, u):
    rows = 256
    return pl.pallas_call(
        update_kernel,
        grid=(SIDE // rows,),
        out_shape=jax.ShapeDtypeStruct((SIDE, SIDE), jnp.float32),
        in_specs=[
            pl.BlockSpec((rows, SIDE), lambda i: (i, 0)),
            pl.BlockSpec((rows, 2 * TILE), lambda i: (i, 0)),
            pl.BlockSpec((2 * TILE, SIDE), lambda i: (0, 0)),
            pl.BlockSpec((2 * TILE, SIDE), lambda i: (0, 0)),
            pl.BlockSpec((2, TILE, TILE), lambda i: (0, 0, 0)),
        ],
        out_specs=pl.BlockSpec((rows, SIDE), lambda i: (i, 0)),
        compiler_params=pltpu.CompilerParams(vmem_limit_bytes=40 * 2**20),
        name="update",
    )(matrix, pr, pc_hi, pc_lo, u)


def per_device(matrix):
    return update(matrix, *panels(matrix))


def solution(mesh):
    return jax.shard_map(
        per_device, mesh=mesh, in_specs=(P("row", "col"),), out_specs=P("row", "col"),
        check_vma=False,
    )
```

time: 732 us -> 93.5 us (0.13)
  waiting for transfers between devices: 576 us -> 0 us
  Pallas kernels: 0 us -> 90.6 us
  other arithmetic: 60.6 us -> 0 us
  local copies, waits for them, and re-layouts: 51.7 us -> 2.86 us
  matrix products: 24.1 us -> 0 us
  between operations: 13.7 us -> 0.01 us
    psum x4 -> x0, waiting for transfers between devices: 395 us -> none  [spread(): return lax.psum(block, axis)]
    all_gather x2 -> x0, waiting for transfers between devices: 181 us -> none  [gathered_columns(): whole = lax.all_gather(rows_panel, 'row', axis=0, tiled=True)]
    pallas_call x0 -> x2, Pallas kernels: none -> 90.6 us  [the longest x1 85.3 us: panels(): pl.pallas_call(panels_kernel, out_shape=[jax.ShapeDtypeStruct((SIDE, 2 *...]
    another operation x11 -> x0, other arithmetic: 46.7 us -> none  [the longest x6 24.9 us: factor_panel(): lower = jnp.linalg.cholesky(corner)]
    dot_general x4 -> x0, matrix products: 23.6 us -> none  [product_t(): lax.dot_general(left, right, (((1,), (1,)), ((), ())), precision=lax.Prec...]
    reshape x2 -> x0, local copies, waits for them, and re-layouts: 23.5 us -> none  [gathered_columns(): blocks = whole.reshape(row_count * row_tiles, tile, tile)]
    scatter x4 -> x0, other arithmetic: 9.84 us -> none  [the longest x2 5.42 us: finish_panel(): work.at[:, start:start + tile]]
    gather x2 -> x0, local copies, waits for them, and re-layouts: 9.13 us -> none  [gathered_columns(): return jnp.take(blocks, tile_index, axis=0).reshape(-1, tile)]
  transfers between devices with their start and end apart: 6 -> 0, of which waited for: 6 -> 0; matrix products, arithmetic and copies ran while one was open for 0% -> 0% of each run, Pallas kernels for 0% -> 0%
where the time goes in v1:
time: 93.5 us; the launch traced here: 93.4 us
  Pallas kernels  90.6 us (97%)
  local copies, waits for them, and re-layouts  2.86 us (3%)
    pallas_call x1, Pallas kernels, panels(): pl.pallas_call(panels_kernel, out_shape=[jax.ShapeDtypeStruct((SIDE, 2 *...  85.3 us
    pallas_call x1, Pallas kernels, update(): pl.pallas_call(update_kernel, grid=(SIDE // rows,), out_shape=jax.ShapeDt...  5.26 us
    unnamed x2, local copies, waits for them, and re-layouts  2.86 us

profile of v1, /device:TPU:240, one launch (start us, length us, event | category | flops | bytes accessed | tf_op | source)
XLA Modules:
  0.0 93.4 jit_solution(2624441104740254433)
XLA Ops:
  0.0 0.0 copy-start
  0.0 2.9 %copy-done = f32[1280,1280]{1,0:T(8,128)S(1)} copy-done((f32[1280,1280]{1,0:T(8,128)S(1)}, f32[1280,1280]{1,0:T(8,128)}, u32[]{:S(2)}) %copy-start) | copy-done | bytes 6553624
  2.9 85.3 %panels.1 = (f32[1280,256]{1,0:T(8,128)S(1)}, bf16[256,1280]{1,0:T(8,128)(2,1)S(1)}, bf16[256,1280]{1,0:T(8,128)(2,1)S(1)}, f32[2,128,128]{2,1,0:T(8,128)S(1)}) custom-call(f32[1280,1280]{1,0:T(8,128)S(1)} %copy-done), custom_call_target="tpu_custom_call" | custom-call | tf_op jit(solution)/shard_map/panels/pallas_call | solution.py:355
  88.2 5.3 %update.1 = f32[1280,1280]{1,0:T(8,128)} custom-call(f32[1280,1280]{1,0:T(8,128)S(1)} %copy-done, f32[1280,256]{1,0:T(8,128)S(1)} %get-tuple-element.9.pr_ref, bf16[256,1280]{1,0:T(8,128)(2,1)S(1)} %get-tuple-element.10.pc_hi_ref, bf16[256,1280]{1,0:T(8,128)(2,1)S(1)} %get-tuple-element.11.pc_lo_ref, f32[2,128,128]{2,1,0:T(8,128)S(1)} %get-tuple-element.12.u_ref), custom_call_target="tpu_custom_call" | custom-call | tf_op jit(solution)/shard_map/update/pallas_call | solution.py:416
Async XLA Ops:
  0.0 2.9 %copy-start = (f32[1280,1280]{1,0:T(8,128)S(1)}, f32[1280,1280]{1,0:T(8,128)}, u32[]{:S(2)}) copy-start(f32[1280,1280]{1,0:T(8,128)} %a_ref.3) | copy-start | bytes 19660804

commit v2 on v1

v2 whole, which is shorter than its diff:
```python
import functools

import jax
import jax.numpy as jnp
from jax import lax
from jax.experimental import pallas as pl
from jax.experimental.pallas import tpu as pltpu
from jax.sharding import PartitionSpec as P

TILE = 128
SUP = 64
SIDE = 1280
RING_X = 4
RING_Y = 4
RING_Z = 8
ZCH = 8
ZROWS = SIDE // ZCH
PCH = 4
PROWS = TILE // 4 // PCH
FIRST = 18
UROWS = 128
VMEM_LIMIT = 40 * 2**20
UPDATE_LIMIT = 24 * 2**20
EXACT = lax.Precision.HIGHEST
MESH = pl.DeviceIdType.MESH


def dot(left, right, dims):
    return lax.dot_general(
        left, right, (dims, ((), ())), precision=EXACT, preferred_element_type=jnp.float32
    )


def cholesky_inverse(tile):
    sub = lax.broadcasted_iota(jnp.int32, (8, TILE), 0)
    lane = lax.broadcasted_iota(jnp.int32, (8, TILE), 1)
    count = TILE // 8
    a = [tile[8 * i : 8 * i + 8] for i in range(count)]
    w = [jnp.where(lane == sub + 8 * i, 1.0, 0.0) for i in range(count)]
    for start in range(0, TILE, SUP):
        blocks = list(range(start // 8, (start + SUP) // 8))
        for t in blocks:
            j0 = 8 * t
            rest = [m for m in blocks if m >= t]
            col = {
                m: [jnp.broadcast_to(a[m][:, j0 + q : j0 + q + 1], (8, TILE)) for q in range(8)]
                for m in rest
            }
            scale = jnp.zeros((8, TILE), jnp.float32)
            for p in range(8):
                root = lax.rsqrt(jnp.broadcast_to(col[t][p][p : p + 1], (8, TILE)))
                scale = jnp.where(sub == p, root, scale)
                row_a = jnp.broadcast_to(a[t][p : p + 1], (8, TILE)) * root
                row_w = jnp.broadcast_to(w[t][p : p + 1], (8, TILE)) * root
                piece = {
                    q: jnp.broadcast_to(col[t][q][p : p + 1], (8, TILE)) * root
                    for q in range(p + 1, 8)
                }
                for m in rest:
                    factor = col[m][p] * root
                    for q in range(p + 1, 8):
                        col[m][q] = col[m][q] - factor * piece[q]
                    if m == t:
                        factor = jnp.where(sub > p, factor, 0.0)
                    a[m] = a[m] - factor * row_a
                    w[m] = w[m] - factor * row_w
            a[t] = jnp.where(lane >= sub + j0, a[t] * scale, 0.0)
            w[t] = w[t] * scale
        end = start + SUP
        if end < TILE:
            upper = jnp.concatenate([a[m] for m in blocks], 0)
            both = jnp.concatenate([upper, jnp.concatenate([w[m] for m in blocks], 0)], 1)
            change = dot(upper, both, ((0,), (0,)))
            for m in range(end // 8, count):
                a[m] = a[m] - change[8 * m : 8 * m + 8, :TILE]
                w[m] = w[m] - change[8 * m : 8 * m + 8, TILE:]
    return jnp.concatenate(a, 0), jnp.concatenate(w, 0)


def place():
    r = lax.axis_index("row")
    c = lax.axis_index("col")
    return r % RING_X, r // RING_X, c // 2, c % 2


def device(x, y, z, k):
    return (y * RING_X + x, z * 2 + k)


def wrap(i, n):
    return lax.rem(i + n, n)


TREE = {
    (0, 0): (0,), (1, 0): (0, 1, 3), (2, 0): (0, 3), (1, 1): (0, 1, 2), (1, 3): (2,),
    (2, 1): (0, 1), (2, 3): (0,), (1, 2): (2,), (2, 2): (0,),
}
LEVEL = {(0, 0): 0, (1, 0): 1, (2, 0): 2, (1, 1): 2, (1, 3): 2, (2, 1): 3, (2, 3): 3, (1, 2): 3, (2, 2): 4}
STEPS = ((1, 0), (0, 1), (-1, 0), (0, -1))
HOP = 3


def panels_kernel(
    a_ref, a_out, pr_ref, pc_hi_ref, pc_lo_ref,
    hr, hc, cn, w_all,
    cn_recv, cn_send, cn_sib, z_recv, z_send, z_sib_recv, z_sib_send, z_own,
    p_recv, p_send, p_own, a_sem,
):
    x, y, z, k = place()
    r = y * RING_X + x
    sibling = device(x, y, z, 1 - k)
    step = 1 - 2 * k
    pos = jnp.where(k == 0, z, wrap(RING_Z - z, RING_Z))
    around = (
        device(wrap(x + 1, RING_X), y, z, k),
        device(x, wrap(y + 1, RING_Y), z, k),
        device(wrap(x - 1, RING_X), y, z, k),
        device(x, wrap(y - 1, RING_Y), z, k),
    )
    z_next = device(x, y, wrap(z + step, RING_Z), k)
    z_prev = device(x, y, wrap(z - step, RING_Z), k)
    z_skip = device(x, y, wrap(z + 2 * step, RING_Z), k)
    z_back = device(x, y, wrap(z - 2 * step, RING_Z), k)
    x_far = device(wrap(x + 2, RING_X), y, z, k)
    y_far = device(x, wrap(y + 2, RING_Y), z, k)

    pltpu.make_async_copy(a_ref, a_out, a_sem).start()
    barrier = pltpu.get_barrier_semaphore()

    def greet(target):
        pl.semaphore_signal(barrier, inc=1, device_id=target, device_id_type=MESH)

    for target in (sibling, z_next, z_prev, x_far, y_far) + around:
        greet(target)

    @pl.when(pos == 4)
    def _():
        greet(z_back)

    root_core = (0, 1, 1)
    root_x = (0, 0, 1)
    count = 9 + jnp.where(pos == 2, 1, 0)
    for tile in range(3):
        in_ring = jnp.logical_and(jnp.logical_and(x == root_x[tile], y == 0), k == root_core[tile])

        @pl.when(jnp.logical_and(in_ring, z != 0))
        def _(tile=tile):
            greet((root_x[tile], root_core[tile]))

        count = count + jnp.where(jnp.logical_and(in_ring, z == 0), 7, 0)
    pl.semaphore_wait(barrier, count)

    def remote(src, dst, send, recv, target):
        return pltpu.make_async_remote_copy(
            src_ref=src, dst_ref=dst, send_sem=send, recv_sem=recv, device_id=target,
            device_id_type=MESH,
        )

    corner_src = a_ref.at[0:TILE, 0:TILE]

    def corner_z(tile):
        mine = jnp.logical_and(jnp.logical_and(x == root_x[tile], y == 0), k == root_core[tile])

        @pl.when(jnp.logical_and(mine, z == 0))
        def _():
            for i in range(1, RING_Z):
                remote(
                    corner_src, cn.at[tile], cn_send.at[tile, i - 1], cn_recv.at[tile],
                    (root_x[tile], i * 2 + root_core[tile]),
                ).start()
            pltpu.make_async_copy(corner_src, cn.at[tile], cn_recv.at[tile]).start()

    def corner_wait(tile):
        pltpu.make_async_copy(corner_src, cn.at[tile], cn_recv.at[tile]).wait()

    def corner_send(tile, sem, target):
        remote(cn.at[tile], cn.at[tile], cn_send.at[tile, sem], cn_recv.at[tile], target).start()

    def corner_x(tile):
        mine = jnp.logical_and(jnp.logical_and(x == root_x[tile], y == 0), k == root_core[tile])

        @pl.when(mine)
        def _():
            corner_wait(tile)
            corner_send(tile, 7, around[0])
            corner_send(tile, 8, around[2])
            corner_send(tile, 9, x_far)
            corner_send(tile, 10, around[1])
            corner_send(tile, 11, around[3])
            corner_send(tile, 12, y_far)
            remote(cn.at[tile], cn.at[tile], cn_sib.at[tile], cn_recv.at[tile], sibling).start()

    def corner_y(tile):
        mine = jnp.logical_and(k == root_core[tile], jnp.logical_and(y == 0, x != root_x[tile]))

        @pl.when(mine)
        def _():
            corner_wait(tile)
            corner_send(tile, 10, around[1])
            corner_send(tile, 11, around[3])
            corner_send(tile, 12, y_far)
            remote(cn.at[tile], cn.at[tile], cn_sib.at[tile], cn_recv.at[tile], sibling).start()

    def corner_end(tile):
        @pl.when(jnp.logical_and(k == root_core[tile], y != 0))
        def _():
            corner_wait(tile)
            remote(cn.at[tile], cn.at[tile], cn_sib.at[tile], cn_recv.at[tile], sibling).start()

        @pl.when(k != root_core[tile])
        def _():
            corner_wait(tile)

    def corner_drain(tile):
        mine = k == root_core[tile]
        here = cn.at[tile]

        def sent(sem):
            remote(here, here, sem, cn_recv.at[tile], sibling).wait_send()

        @pl.when(mine)
        def _():
            sent(cn_sib.at[tile])

            @pl.when(y == 0)
            def _():
                for i in (10, 11, 12):
                    sent(cn_send.at[tile, i])

            @pl.when(jnp.logical_and(y == 0, x == root_x[tile]))
            def _():
                for i in (7, 8, 9):
                    sent(cn_send.at[tile, i])

                @pl.when(z == 0)
                def _():
                    for i in range(7):
                        sent(cn_send.at[tile, i])

    def z_rows(j):
        return pl.ds(j * ZROWS, ZROWS)

    def z_send_chunk(j, way, src, target):
        remote(src, hr.at[k, z_rows(j)], z_send.at[way], z_recv.at[j], target).start()

    def z_sibling(j, src):
        remote(src, hr.at[k, z_rows(j)], z_sib_send, z_sib_recv, sibling).start()

    def z_service(j, place_here):
        @pl.when(pos == place_here)
        def _():
            here = hr.at[k, z_rows(j)]
            pltpu.make_async_copy(here, here, z_recv.at[j]).wait()
            if place_here in (1, 2, 4):
                z_send_chunk(j, 0, here, z_next)
            if place_here == 2:
                z_send_chunk(j, 1, here, z_skip)
            if place_here == 7:
                z_send_chunk(j, 0, here, z_prev)
            z_sibling(j, here)

    whole_r = hr.at[k]

    def z_sent(way):
        remote(whole_r, whole_r, z_send.at[way], z_sib_recv, sibling).wait_send()

    trees = []
    for s in range(2):
        for d in range(4):
            fx, fy = wrap(x - s + RING_X, RING_X), y
            for _ in range(d):
                fx, fy = fy, wrap(RING_X - fx, RING_X)
            at = fx + RING_X * fy
            trees.append((s, d, at))

    def p_rows(d, j):
        start = d * (TILE // 4) + j * PROWS
        return slice(start, start + PROWS)

    def p_service(index, j, level):
        s, d, at = trees[index]
        here = hc.at[s, p_rows(d, j)]
        for spot, ways in TREE.items():
            if LEVEL[spot] != level:
                continue

            @pl.when(at == spot[0] + RING_X * spot[1])
            def _(ways=ways):
                if level == 0:
                    src = a_ref.at[p_rows(d, j)]
                else:
                    src = here
                    pltpu.make_async_copy(here, here, p_recv.at[index, j]).wait()
                for way in ways:
                    remote(
                        src, here, p_send.at[index, way], p_recv.at[index, j],
                        around[(way + d) % 4],
                    ).start()

    def p_end(index):
        s, d, at = trees[index]
        inner = [spot[0] + RING_X * spot[1] for spot in TREE]
        leaf = at != inner[0]
        for spot in inner[1:]:
            leaf = jnp.logical_and(leaf, at != spot)
        for j in range(PCH):
            here = hc.at[s, p_rows(d, j)]

            @pl.when(leaf)
            def _(here=here, j=j):
                pltpu.make_async_copy(here, here, p_recv.at[index, j]).wait()

    def p_drain(index):
        s, d, at = trees[index]
        part = hc.at[s, d * (TILE // 4) : (d + 1) * (TILE // 4)]
        for spot, ways in TREE.items():

            @pl.when(at == spot[0] + RING_X * spot[1])
            def _(ways=ways):
                for way in ways:
                    remote(
                        part, part, p_send.at[index, way], p_recv.at[index, 0], sibling
                    ).wait_send()

    for tile in range(3):
        corner_z(tile)

    @pl.when(pos == 0)
    def _():
        for j in range(ZCH):
            z_send_chunk(j, 0, a_ref.at[z_rows(j), 0:TILE], z_next)
        for j in range(ZCH):
            z_sibling(j, a_ref.at[z_rows(j), 0:TILE])
        pltpu.make_async_copy(a_ref.at[:, 0:TILE], hr.at[k], z_own).start()

    for j in range(PCH):
        for index in range(8):
            p_service(index, j, 0)

    @pl.when(r < 2)
    def _():
        pltpu.make_async_copy(a_ref.at[0:TILE, :], hc.at[r], p_own).start()

    def second_wave():
        @pl.when(pos == 0)
        def _():
            z_sent(0)
            for j in range(ZCH):
                z_send_chunk(j, 1, a_ref.at[z_rows(j), 0:TILE], z_prev)

    z_level = {1: 0, 2: 1, 3: 2, 4: 2, 5: 3, 7: 3, 6: 4}
    def slot_work(slot):
        if slot == 4:
            for tile in range(3):
                corner_x(tile)
        if slot == 7:
            second_wave()
        if slot == 8:
            for tile in range(3):
                corner_y(tile)
        for j in range(PCH):
            for level in range(1, 5):
                if HOP * level + 2 * j == slot:
                    for index in range(8):
                        p_service(index, j, level)
        for j in range(ZCH):
            for where_, level in ((1, 1), (2, 2), (3, 3), (4, 3), (5, 4)):
                if HOP * level + j == slot:
                    z_service(j, where_)
            for where_, level in ((7, 1), (6, 2)):
                if 8 + HOP * level + j == slot:
                    z_service(j, where_)

    for slot in range(1, FIRST):
        slot_work(slot)

    corner_end(0)
    u0, w0 = cholesky_inverse(cn[0])
    w_all[:TILE, :TILE] = w0
    w_all[:TILE, TILE:] = jnp.zeros((TILE, TILE), jnp.float32)
    corner_end(1)
    corner_end(2)
    u01 = dot(w_all[:TILE, :TILE], cn[1], ((1,), (0,)))
    for slot in range(FIRST, 25):
        slot_work(slot)
    u1, w1 = cholesky_inverse(cn[2] - dot(u01, u01, ((0,), (0,))))
    w10 = -dot(w1, dot(u01, w_all[:TILE, :TILE], ((0,), (0,))), ((1,), (0,)))
    w_all[TILE:, :TILE] = w10
    w_all[TILE:, TILE:] = w1

    other_r = hr.at[1 - k]
    pltpu.make_async_copy(other_r, other_r, z_sib_recv).wait()

    @pl.when(pos == 0)
    def _():
        pltpu.make_async_copy(a_ref.at[:, 0:TILE], hr.at[k], z_own).wait()

    @pl.when(r < 2)
    def _():
        pltpu.make_async_copy(a_ref.at[0:TILE, :], hc.at[r], p_own).wait()

    for index in range(8):
        p_end(index)

    @pl.loop(0, SIDE // 256)
    def _(i):
        rows = pl.ds(pl.multiple_of(i * 256, 256), 256)
        raw = jnp.concatenate([hr[0, rows], hr[1, rows]], axis=1)
        pr_ref[rows] = dot(raw, w_all[...], ((1,), (1,)))

    for i in range(SIDE // 256):
        lanes = slice(i * 256, i * 256 + 256)
        raw = jnp.concatenate([hc[0, :, lanes], hc[1, :, lanes]], axis=0)
        got = dot(w_all[...], raw, ((1,), (0,)))
        high = got.astype(jnp.bfloat16)
        pc_hi_ref[:, lanes] = high
        pc_lo_ref[:, lanes] = (got - high.astype(jnp.float32)).astype(jnp.bfloat16)

    for tile in range(3):
        corner_drain(tile)
    remote(whole_r, whole_r, z_sib_send, z_sib_recv, sibling).wait_send()

    @pl.when(jnp.logical_or(jnp.logical_or(pos == 1, pos == 2), jnp.logical_or(pos == 4, pos == 7)))
    def _():
        z_sent(0)

    @pl.when(jnp.logical_or(pos == 0, pos == 2))
    def _():
        z_sent(1)

    for index in range(8):
        p_drain(index)
    pltpu.make_async_copy(a_ref, a_out, a_sem).wait()


def panels(matrix):
    vmem = pl.BlockSpec(memory_space=pltpu.VMEM)
    f32 = jnp.float32
    dma = pltpu.SemaphoreType.DMA
    return pl.pallas_call(
        panels_kernel,
        out_shape=[
            pltpu.VMEM((SIDE, SIDE), f32),
            pltpu.VMEM((SIDE, 2 * TILE), f32),
            pltpu.VMEM((2 * TILE, SIDE), jnp.bfloat16),
            pltpu.VMEM((2 * TILE, SIDE), jnp.bfloat16),
        ],
        in_specs=[pl.BlockSpec(memory_space=pl.ANY)],
        out_specs=[vmem] * 4,
        scratch_shapes=[
            pltpu.VMEM((2, SIDE, TILE), f32),
            pltpu.VMEM((2, TILE, SIDE), f32),
            pltpu.VMEM((3, TILE, TILE), f32),
            pltpu.VMEM((2 * TILE, 2 * TILE), f32),
            dma((3,)), dma((3, 13)), dma((3,)),
            dma((ZCH,)), dma((2,)), dma, dma, dma,
            dma((8, PCH)), dma((8, 4)), dma, dma,
        ],
        compiler_params=pltpu.CompilerParams(
            collective_id=0, has_side_effects=True, vmem_limit_bytes=VMEM_LIMIT
        ),
        name="panels",
    )(matrix)


def update_kernel(a_ref, pr_ref, pc_hi_ref, pc_lo_ref, out_ref, stage, sem):
    r = lax.axis_index("row")
    c = lax.axis_index("col")

    def part(left, right):
        return lax.dot_general(
            left, right[...], (((1,), (0,)), ((), ())), preferred_element_type=jnp.float32
        )

    for i in range(SIDE // UROWS):
        rows = slice(i * UROWS, (i + 1) * UROWS)
        high = pr_ref[rows].astype(jnp.bfloat16)
        low = (pr_ref[rows] - high.astype(jnp.float32)).astype(jnp.bfloat16)
        stage[rows] = a_ref[rows] - (
            part(high, pc_hi_ref) + (part(high, pc_lo_ref) + part(low, pc_hi_ref))
        )

        @pl.when(c == 0)
        def _(rows=rows):
            stage[rows, :TILE] = pr_ref[rows, :TILE]

        @pl.when(c == 1)
        def _(rows=rows):
            stage[rows, :TILE] = pr_ref[rows, TILE:]

        if i == 0:

            @pl.when(r < 2)
            def _():
                row = lax.broadcasted_iota(jnp.int32, (TILE, TILE), 0)
                lane = lax.broadcasted_iota(jnp.int32, (TILE, TILE), 1)
                kept = jnp.logical_or(c < r, jnp.logical_and(c == r, lane <= row))
                stage[:TILE, :TILE] = jnp.where(kept, stage[:TILE, :TILE], 0.0)
                stage[:TILE, TILE:] = jnp.zeros((TILE, SIDE - TILE), jnp.float32)

        pltpu.make_async_copy(stage.at[rows], out_ref.at[rows], sem.at[i]).start()
    for i in range(SIDE // UROWS):
        rows = slice(i * UROWS, (i + 1) * UROWS)
        pltpu.make_async_copy(stage.at[rows], out_ref.at[rows], sem.at[i]).wait()


def update(a, pr, pc_hi, pc_lo):
    vmem = pl.BlockSpec(memory_space=pltpu.VMEM)
    return pl.pallas_call(
        update_kernel,
        out_shape=jax.ShapeDtypeStruct((SIDE, SIDE), jnp.float32),
        in_specs=[vmem] * 4,
        out_specs=pl.BlockSpec(memory_space=pl.ANY),
        scratch_shapes=[
            pltpu.VMEM((SIDE, SIDE), jnp.float32), pltpu.SemaphoreType.DMA((SIDE // UROWS,)),
        ],
        compiler_params=pltpu.CompilerParams(vmem_limit_bytes=UPDATE_LIMIT),
        name="update",
    )(a, pr, pc_hi, pc_lo)


def per_device(matrix):
    return update(*panels(matrix))


def solution(mesh):
    return jax.shard_map(
        per_device, mesh=mesh, in_specs=(P("row", "col"),), out_specs=P("row", "col"),
        check_vma=False,
    )
```

time: 93.5 us -> 53.1 us (0.57)
  the two profiles are of different devices: /device:TPU:240 before, /device:TPU:128 now
where the time goes in v2:
time: 53.1 us; the launch traced here: 53 us
  Pallas kernels  52.9 us (100%)
    pallas_call x1, Pallas kernels, panels(): pl.pallas_call(panels_kernel, out_shape=[pltpu.VMEM((SIDE, SIDE), f32), p...  45.3 us
    pallas_call x1, Pallas kernels, update(): pl.pallas_call(update_kernel, out_shape=jax.ShapeDtypeStruct((SIDE, SIDE)...  7.56 us

profile of v2, /device:TPU:128, one launch (start us, length us, event | category | flops | bytes accessed | tf_op | source)
XLA Modules:
  0.0 53.0 jit_solution(1452618160742972481)
XLA Ops:
  0.0 45.3 %panels.1 = (f32[1280,1280]{1,0:T(8,128)S(1)}, f32[1280,256]{1,0:T(8,128)S(1)}, bf16[256,1280]{1,0:T(8,128)(2,1)S(1)}, bf16[256,1280]{1,0:T(8,128)(2,1)S(1)}) custom-call(f32[1280,1280]{1,0:T(8,128)} %a_ref.1), custom_call_target="tpu_custom_call" | custom-call | tf_op jit(solution)/shard_map/panels/pallas_call | solution.py:440
  45.3 7.6 %update.1 = f32[1280,1280]{1,0:T(8,128)} custom-call(f32[1280,1280]{1,0:T(8,128)S(1)} %get-tuple-element.9.a_ref, f32[1280,256]{1,0:T(8,128)S(1)} %get-tuple-element.10.pr_ref, bf16[256,1280]{1,0:T(8,128)(2,1)S(1)} %get-tuple-element.11.pc_hi_ref, bf16[256,1280]{1,0:T(8,128)(2,1)S(1)} %get-tuple-element.12.pc_lo_ref), custom_call_target="tpu_custom_call" | custom-call | tf_op jit(solution)/shard_map/update/pallas_call | solution.py:509

commit v3 on v2

--- a/solution.py
+++ b/solution.py
@@ -13,12 +13,15 @@
 RING_X = 4
 RING_Y = 4
 RING_Z = 8
-ZCH = 8
+ZCH = 16
 ZROWS = SIDE // ZCH
 PCH = 4
 PROWS = TILE // 4 // PCH
-FIRST = 18
-UROWS = 128
+FIRST = 11
+CX = {4: (0,), 7: (1, 2)}
+CY = {8: (0,), 11: (1, 2)}
+PC_SLOT = 20
+PER_SLOT = 3
 VMEM_LIMIT = 40 * 2**20
 UPDATE_LIMIT = 24 * 2**20
 EXACT = lax.Precision.HIGHEST
@@ -29,6 +32,19 @@
     return lax.dot_general(
         left, right, (dims, ((), ())), precision=EXACT, preferred_element_type=jnp.float32
     )
+
+
+def panel_dot(left, right, dims):
+    def split(value):
+        high = value.astype(jnp.bfloat16)
+        return high, (value - high.astype(jnp.float32)).astype(jnp.bfloat16)
+
+    def part(a, b):
+        return lax.dot_general(a, b, (dims, ((), ())), preferred_element_type=jnp.float32)
+
+    left_high, left_low = split(left)
+    right_high, right_low = split(right)
+    return part(left_high, right_high) + (part(left_high, right_low) + part(left_low, right_high))
 
 
 def cholesky_inverse(tile):
@@ -64,8 +80,9 @@
                         factor = jnp.where(sub > p, factor, 0.0)
                     a[m] = a[m] - factor * row_a
                     w[m] = w[m] - factor * row_w
-            a[t] = jnp.where(lane >= sub + j0, a[t] * scale, 0.0)
+            a[t] = a[t] * scale
             w[t] = w[t] * scale
+            yield
         end = start + SUP
         if end < TILE:
             upper = jnp.concatenate([a[m] for m in blocks], 0)
@@ -74,7 +91,8 @@
             for m in range(end // 8, count):
                 a[m] = a[m] - change[8 * m : 8 * m + 8, :TILE]
                 w[m] = w[m] - change[8 * m : 8 * m + 8, TILE:]
-    return jnp.concatenate(a, 0), jnp.concatenate(w, 0)
+            yield
+    return jnp.concatenate(w, 0)
 
 
 def place():
@@ -93,11 +111,12 @@
 
 TREE = {
     (0, 0): (0,), (1, 0): (0, 1, 3), (2, 0): (0, 3), (1, 1): (0, 1, 2), (1, 3): (2,),
-    (2, 1): (0, 1), (2, 3): (0,), (1, 2): (2,), (2, 2): (0,),
+    (2, 1): (0, 1, 4), (2, 3): (0,), (1, 2): (2,),
 }
-LEVEL = {(0, 0): 0, (1, 0): 1, (2, 0): 2, (1, 1): 2, (1, 3): 2, (2, 1): 3, (2, 3): 3, (1, 2): 3, (2, 2): 4}
+LEVEL = {(0, 0): 0, (1, 0): 1, (2, 0): 2, (1, 1): 2, (1, 3): 2, (2, 1): 3, (2, 3): 3, (1, 2): 3}
 STEPS = ((1, 0), (0, 1), (-1, 0), (0, -1))
 HOP = 3
+Z_FAN = {0: (2, 6), 2: (1, 3, 4), 6: (5, 7)}
 
 
 def panels_kernel(
@@ -117,6 +136,10 @@
         device(wrap(x - 1, RING_X), y, z, k),
         device(x, wrap(y - 1, RING_Y), z, k),
     )
+    corners = tuple(
+        device(wrap(x + dx, RING_X), wrap(y + dy, RING_Y), z, k)
+        for dx, dy in ((1, 1), (-1, 1), (-1, -1), (1, -1))
+    )
     z_next = device(x, y, wrap(z + step, RING_Z), k)
     z_prev = device(x, y, wrap(z - step, RING_Z), k)
     z_skip = device(x, y, wrap(z + 2 * step, RING_Z), k)
@@ -130,24 +153,34 @@
     def greet(target):
         pl.semaphore_signal(barrier, inc=1, device_id=target, device_id_type=MESH)
 
-    for target in (sibling, z_next, z_prev, x_far, y_far) + around:
+    for target in (sibling, z_next, z_prev, x_far, y_far) + around + corners:
         greet(target)
 
     @pl.when(pos == 4)
     def _():
         greet(z_back)
 
-    root_core = (0, 1, 1)
-    root_x = (0, 0, 1)
-    count = 9 + jnp.where(pos == 2, 1, 0)
+    root_core = (0, 0, 1)
+    root_x = (0, 1, 1)
+    count = 13 + jnp.where(pos == 2, 1, 0)
     for tile in range(3):
         in_ring = jnp.logical_and(jnp.logical_and(x == root_x[tile], y == 0), k == root_core[tile])
 
-        @pl.when(jnp.logical_and(in_ring, z != 0))
-        def _(tile=tile):
-            greet((root_x[tile], root_core[tile]))
-
-        count = count + jnp.where(jnp.logical_and(in_ring, z == 0), 7, 0)
+        def greet_ring(where_, place_z, tile=tile, in_ring=in_ring):
+            @pl.when(jnp.logical_and(in_ring, where_))
+            def _():
+                greet((root_x[tile], place_z * 2 + root_core[tile]))
+
+        if tile == 0:
+            greet_ring(z != 0, 0)
+            count = count + jnp.where(jnp.logical_and(in_ring, z == 0), 7, 0)
+        else:
+            greet_ring(jnp.logical_or(z == 2, z == 6), 0)
+            greet_ring(jnp.logical_or(z == 1, jnp.logical_or(z == 3, z == 4)), 2)
+            greet_ring(jnp.logical_or(z == 5, z == 7), 6)
+            fan = jnp.where(z == 2, 3, jnp.where(jnp.logical_or(z == 0, z == 6), 2, 0))
+            count = count + jnp.where(in_ring, fan, 0)
+
     pl.semaphore_wait(barrier, count)
 
     def remote(src, dst, send, recv, target):
@@ -163,10 +196,11 @@
 
         @pl.when(jnp.logical_and(mine, z == 0))
         def _():
-            for i in range(1, RING_Z):
+            targets = Z_FAN[0] if tile else tuple(range(1, RING_Z))
+            for i, to in enumerate(targets):
                 remote(
-                    corner_src, cn.at[tile], cn_send.at[tile, i - 1], cn_recv.at[tile],
-                    (root_x[tile], i * 2 + root_core[tile]),
+                    corner_src, cn.at[tile], cn_send.at[tile, i],
+                    cn_recv.at[tile], (root_x[tile], to * 2 + root_core[tile]),
                 ).start()
             pltpu.make_async_copy(corner_src, cn.at[tile], cn_recv.at[tile]).start()
 
@@ -182,6 +216,14 @@
         @pl.when(mine)
         def _():
             corner_wait(tile)
+            if tile:
+                for place_z in (2, 6):
+
+                    @pl.when(z == place_z)
+                    def _(place_z=place_z):
+                        for i, to in enumerate(Z_FAN[place_z]):
+                            corner_send(tile, i, (root_x[tile], to * 2 + root_core[tile]))
+
             corner_send(tile, 7, around[0])
             corner_send(tile, 8, around[2])
             corner_send(tile, 9, x_far)
@@ -232,10 +274,12 @@
                 for i in (7, 8, 9):
                     sent(cn_send.at[tile, i])
 
-                @pl.when(z == 0)
-                def _():
-                    for i in range(7):
-                        sent(cn_send.at[tile, i])
+                for place_z in (0, 2, 6) if tile else (0,):
+
+                    @pl.when(z == place_z)
+                    def _(place_z=place_z):
+                        for i in range(len(Z_FAN[place_z]) if tile else 7):
+                            sent(cn_send.at[tile, i])
 
     def z_rows(j):
         return pl.ds(j * ZROWS, ZROWS)
@@ -244,7 +288,7 @@
         remote(src, hr.at[k, z_rows(j)], z_send.at[way], z_recv.at[j], target).start()
 
     def z_sibling(j, src):
-        remote(src, hr.at[k, z_rows(j)], z_sib_send, z_sib_recv, sibling).start()
+        remote(src, hr.at[k, z_rows(j)], z_sib_send, z_sib_recv.at[j], sibling).start()
 
     def z_service(j, place_here):
         @pl.when(pos == place_here)
@@ -262,7 +306,7 @@
     whole_r = hr.at[k]
 
     def z_sent(way):
-        remote(whole_r, whole_r, z_send.at[way], z_sib_recv, sibling).wait_send()
+        remote(whole_r, whole_r, z_send.at[way], z_sib_recv.at[0], sibling).wait_send()
 
     trees = []
     for s in range(2):
@@ -277,47 +321,58 @@
         start = d * (TILE // 4) + j * PROWS
         return slice(start, start + PROWS)
 
+    def among(at, spots):
+        found = at == spots[0][0] + RING_X * spots[0][1]
+        for spot in spots[1:]:
+            found = jnp.logical_or(found, at == spot[0] + RING_X * spot[1])
+        return found
+
     def p_service(index, j, level):
         s, d, at = trees[index]
         here = hc.at[s, p_rows(d, j)]
-        for spot, ways in TREE.items():
-            if LEVEL[spot] != level:
-                continue
-
-            @pl.when(at == spot[0] + RING_X * spot[1])
-            def _(ways=ways):
-                if level == 0:
-                    src = a_ref.at[p_rows(d, j)]
-                else:
-                    src = here
-                    pltpu.make_async_copy(here, here, p_recv.at[index, j]).wait()
-                for way in ways:
-                    remote(
-                        src, here, p_send.at[index, way], p_recv.at[index, j],
-                        around[(way + d) % 4],
-                    ).start()
+        spots = [spot for spot in TREE if LEVEL[spot] == level]
+
+        @pl.when(among(at, spots))
+        def _():
+            if level == 0:
+                src = a_ref.at[p_rows(d, j)]
+            else:
+                src = here
+                pltpu.make_async_copy(here, here, p_recv.at[index, j]).wait()
+            for way in range(5):
+                users = [spot for spot in spots if way in TREE[spot]]
+                if users:
+
+                    def send(way=way):
+                        remote(
+                            src, here, p_send.at[index, way], p_recv.at[index, j],
+                            corners[d] if way == 4 else around[(way + d) % 4],
+                        ).start()
+
+                    if len(users) == len(spots):
+                        send()
+                    else:
+                        pl.when(among(at, users))(send)
 
     def p_end(index):
         s, d, at = trees[index]
-        inner = [spot[0] + RING_X * spot[1] for spot in TREE]
-        leaf = at != inner[0]
-        for spot in inner[1:]:
-            leaf = jnp.logical_and(leaf, at != spot)
-        for j in range(PCH):
-            here = hc.at[s, p_rows(d, j)]
-
-            @pl.when(leaf)
-            def _(here=here, j=j):
+
+        @pl.when(jnp.logical_not(among(at, list(TREE))))
+        def _():
+            for j in range(PCH):
+                here = hc.at[s, p_rows(d, j)]
                 pltpu.make_async_copy(here, here, p_recv.at[index, j]).wait()
 
     def p_drain(index):
         s, d, at = trees[index]
         part = hc.at[s, d * (TILE // 4) : (d + 1) * (TILE // 4)]
-        for spot, ways in TREE.items():
-
-            @pl.when(at == spot[0] + RING_X * spot[1])
-            def _(ways=ways):
-                for way in ways:
+
+        @pl.when(among(at, list(TREE)))
+        def _():
+            for way in range(5):
+
+                @pl.when(among(at, [spot for spot in TREE if way in TREE[spot]]))
+                def _(way=way):
                     remote(
                         part, part, p_send.at[index, way], p_recv.at[index, 0], sibling
                     ).wait_send()
@@ -350,75 +405,97 @@
 
     z_level = {1: 0, 2: 1, 3: 2, 4: 2, 5: 3, 7: 3, 6: 4}
     def slot_work(slot):
-        if slot == 4:
-            for tile in range(3):
+        if slot in CX:
+            for tile in CX[slot]:
                 corner_x(tile)
         if slot == 7:
             second_wave()
-        if slot == 8:
-            for tile in range(3):
+        if slot in CY:
+            for tile in CY[slot]:
                 corner_y(tile)
+        for j in range(ZCH):
+            for where_, level in ((1, 1), (2, 2), (3, 3), (4, 3), (5, 4)):
+                if HOP * level + j * 8 // ZCH == slot:
+                    z_service(j, where_)
+            for where_, level in ((7, 1), (6, 2)):
+                if 8 + HOP * level + j * 8 // ZCH == slot:
+                    z_service(j, where_)
         for j in range(PCH):
-            for level in range(1, 5):
+            for level in range(1, 4):
                 if HOP * level + 2 * j == slot:
                     for index in range(8):
                         p_service(index, j, level)
+
+    def chain():
+        corner_end(0)
+        w0 = yield from cholesky_inverse(cn[0])
+        w_all[:TILE, :TILE] = w0
+        w_all[:TILE, TILE:] = jnp.zeros((TILE, TILE), jnp.float32)
+        corner_end(1)
+        corner_end(2)
+        u01 = dot(w0, cn[1], ((1,), (1,)))
+        w_all[TILE:, :TILE] = dot(u01, w0, ((0,), (0,)))
+        yield
+        w1 = yield from cholesky_inverse(cn[2] - dot(u01, u01, ((0,), (0,))))
+        w_all[TILE:, TILE:] = w1
+        w_all[TILE:, :TILE] = -dot(w1, w_all[TILE:, :TILE], ((1,), (0,)))
+
+    def columns():
+        @pl.when(r < 2)
+        def _():
+            pltpu.make_async_copy(a_ref.at[0:TILE, :], hc.at[r], p_own).wait()
+
+        for index in range(8):
+            p_end(index)
+        for i in range(SIDE // 256):
+            lanes = slice(i * 256, i * 256 + 256)
+            raw = jnp.concatenate([hc[0, :, lanes], hc[1, :, lanes]], axis=0)
+            got = panel_dot(w_all[...], raw, ((1,), (0,)))
+            high = got.astype(jnp.bfloat16)
+            pc_hi_ref[:, lanes] = high
+            pc_lo_ref[:, lanes] = (got - high.astype(jnp.float32)).astype(jnp.bfloat16)
+
+        @pl.when(pos == 0)
+        def _():
+            pltpu.make_async_copy(a_ref.at[:, 0:TILE], hr.at[k], z_own).wait()
+
+        pltpu.make_async_copy(a_ref, a_out, a_sem).wait()
+
+    def rows_done():
         for j in range(ZCH):
-            for where_, level in ((1, 1), (2, 2), (3, 3), (4, 3), (5, 4)):
-                if HOP * level + j == slot:
-                    z_service(j, where_)
-            for where_, level in ((7, 1), (6, 2)):
-                if 8 + HOP * level + j == slot:
-                    z_service(j, where_)
-
-    for slot in range(1, FIRST):
+            other = hr.at[1 - k, z_rows(j)]
+            pltpu.make_async_copy(other, other, z_sib_recv.at[j]).wait()
+        for i in range(SIDE // 256):
+            rows = slice(i * 256, i * 256 + 256)
+            raw = jnp.concatenate([hr[0, rows], hr[1, rows]], axis=1)
+            pr_ref[rows] = panel_dot(raw, w_all[...], ((1,), (1,)))
+
+    def work():
+        yield from chain()
+        yield
+        while len(slots_seen) < PC_SLOT:
+            yield
+        columns()
+        yield
+        while len(slots_seen) < 50:
+            yield
+        rows_done()
+
+    slots_seen = []
+    steps = work()
+    for slot in range(1, 23):
+        slots_seen.append(slot)
         slot_work(slot)
-
-    corner_end(0)
-    u0, w0 = cholesky_inverse(cn[0])
-    w_all[:TILE, :TILE] = w0
-    w_all[:TILE, TILE:] = jnp.zeros((TILE, TILE), jnp.float32)
-    corner_end(1)
-    corner_end(2)
-    u01 = dot(w_all[:TILE, :TILE], cn[1], ((1,), (0,)))
-    for slot in range(FIRST, 25):
-        slot_work(slot)
-    u1, w1 = cholesky_inverse(cn[2] - dot(u01, u01, ((0,), (0,))))
-    w10 = -dot(w1, dot(u01, w_all[:TILE, :TILE], ((0,), (0,))), ((1,), (0,)))
-    w_all[TILE:, :TILE] = w10
-    w_all[TILE:, TILE:] = w1
-
-    other_r = hr.at[1 - k]
-    pltpu.make_async_copy(other_r, other_r, z_sib_recv).wait()
-
-    @pl.when(pos == 0)
-    def _():
-        pltpu.make_async_copy(a_ref.at[:, 0:TILE], hr.at[k], z_own).wait()
-
-    @pl.when(r < 2)
-    def _():
-        pltpu.make_async_copy(a_ref.at[0:TILE, :], hc.at[r], p_own).wait()
-
-    for index in range(8):
-        p_end(index)
-
-    @pl.loop(0, SIDE // 256)
-    def _(i):
-        rows = pl.ds(pl.multiple_of(i * 256, 256), 256)
-        raw = jnp.concatenate([hr[0, rows], hr[1, rows]], axis=1)
-        pr_ref[rows] = dot(raw, w_all[...], ((1,), (1,)))
-
-    for i in range(SIDE // 256):
-        lanes = slice(i * 256, i * 256 + 256)
-        raw = jnp.concatenate([hc[0, :, lanes], hc[1, :, lanes]], axis=0)
-        got = dot(w_all[...], raw, ((1,), (0,)))
-        high = got.astype(jnp.bfloat16)
-        pc_hi_ref[:, lanes] = high
-        pc_lo_ref[:, lanes] = (got - high.astype(jnp.float32)).astype(jnp.bfloat16)
+        if slot >= FIRST:
+            for _ in range(PER_SLOT):
+                next(steps, None)
+    slots_seen.extend(range(100))
+    for _ in steps:
+        pass
 
     for tile in range(3):
         corner_drain(tile)
-    remote(whole_r, whole_r, z_sib_send, z_sib_recv, sibling).wait_send()
+    remote(whole_r, whole_r, z_sib_send, z_sib_recv.at[0], sibling).wait_send()
 
     @pl.when(jnp.logical_or(jnp.logical_or(pos == 1, pos == 2), jnp.logical_or(pos == 4, pos == 7)))
     def _():
@@ -430,7 +507,6 @@
 
     for index in range(8):
         p_drain(index)
-    pltpu.make_async_copy(a_ref, a_out, a_sem).wait()
 
 
 def panels(matrix):
@@ -453,8 +529,8 @@
             pltpu.VMEM((3, TILE, TILE), f32),
             pltpu.VMEM((2 * TILE, 2 * TILE), f32),
             dma((3,)), dma((3, 13)), dma((3,)),
-            dma((ZCH,)), dma((2,)), dma, dma, dma,
-            dma((8, PCH)), dma((8, 4)), dma, dma,
+            dma((ZCH,)), dma((2,)), dma((ZCH,)), dma, dma,
+            dma((8, PCH)), dma((8, 5)), dma, dma,
         ],
         compiler_params=pltpu.CompilerParams(
             collective_id=0, has_side_effects=True, vmem_limit_bytes=VMEM_LIMIT
@@ -463,7 +539,7 @@
     )(matrix)
 
 
-def update_kernel(a_ref, pr_ref, pc_hi_ref, pc_lo_ref, out_ref, stage, sem):
+def finished(i, raw, panel, pc_hi_ref, pc_lo_ref):
     r = lax.axis_index("row")
     c = lax.axis_index("col")
 
@@ -472,55 +548,50 @@
             left, right[...], (((1,), (0,)), ((), ())), preferred_element_type=jnp.float32
         )
 
-    for i in range(SIDE // UROWS):
-        rows = slice(i * UROWS, (i + 1) * UROWS)
-        high = pr_ref[rows].astype(jnp.bfloat16)
-        low = (pr_ref[rows] - high.astype(jnp.float32)).astype(jnp.bfloat16)
-        stage[rows] = a_ref[rows] - (
-            part(high, pc_hi_ref) + (part(high, pc_lo_ref) + part(low, pc_hi_ref))
-        )
-
-        @pl.when(c == 0)
-        def _(rows=rows):
-            stage[rows, :TILE] = pr_ref[rows, :TILE]
-
-        @pl.when(c == 1)
-        def _(rows=rows):
-            stage[rows, :TILE] = pr_ref[rows, TILE:]
-
-        if i == 0:
-
-            @pl.when(r < 2)
-            def _():
-                row = lax.broadcasted_iota(jnp.int32, (TILE, TILE), 0)
-                lane = lax.broadcasted_iota(jnp.int32, (TILE, TILE), 1)
-                kept = jnp.logical_or(c < r, jnp.logical_and(c == r, lane <= row))
-                stage[:TILE, :TILE] = jnp.where(kept, stage[:TILE, :TILE], 0.0)
-                stage[:TILE, TILE:] = jnp.zeros((TILE, SIDE - TILE), jnp.float32)
-
-        pltpu.make_async_copy(stage.at[rows], out_ref.at[rows], sem.at[i]).start()
-    for i in range(SIDE // UROWS):
-        rows = slice(i * UROWS, (i + 1) * UROWS)
-        pltpu.make_async_copy(stage.at[rows], out_ref.at[rows], sem.at[i]).wait()
-
-
-def update(a, pr, pc_hi, pc_lo):
+    high = panel.astype(jnp.bfloat16)
+    low = (panel - high.astype(jnp.float32)).astype(jnp.bfloat16)
+    full = raw - (part(high, pc_hi_ref) + (part(high, pc_lo_ref) + part(low, pc_hi_ref)))
+    first = jnp.where(c == 0, panel[:, :TILE], jnp.where(c == 1, panel[:, TILE:], full[:, :TILE]))
+    wide = full[:, TILE:]
+    if i == 0:
+        row = lax.broadcasted_iota(jnp.int32, (TILE, TILE), 0)
+        lane = lax.broadcasted_iota(jnp.int32, (TILE, TILE), 1)
+        kept = jnp.logical_or(c < r, jnp.logical_and(c == r, lane <= row))
+        first = jnp.where(jnp.logical_and(r < 2, jnp.logical_not(kept)), 0.0, first)
+        wide = jnp.where(r < 2, 0.0, wide)
+    return first, wide
+
+
+def finish_kernel(a_ref, pr_ref, pc_hi_ref, pc_lo_ref, out_ref, stage, sem):
+    copies = []
+    for i in range(SIDE // TILE):
+        rows = slice(i * TILE, (i + 1) * TILE)
+        first, wide = finished(i, a_ref[rows], pr_ref[rows], pc_hi_ref, pc_lo_ref)
+        stage[rows, :TILE] = first
+        stage[rows, TILE:] = wide
+        copies.append(pltpu.make_async_copy(stage.at[rows], out_ref.at[rows], sem.at[i]))
+        copies[-1].start()
+    for copy in copies:
+        copy.wait()
+
+
+def finish(a, pr, pc_hi, pc_lo):
     vmem = pl.BlockSpec(memory_space=pltpu.VMEM)
     return pl.pallas_call(
-        update_kernel,
+        finish_kernel,
         out_shape=jax.ShapeDtypeStruct((SIDE, SIDE), jnp.float32),
         in_specs=[vmem] * 4,
         out_specs=pl.BlockSpec(memory_space=pl.ANY),
         scratch_shapes=[
-            pltpu.VMEM((SIDE, SIDE), jnp.float32), pltpu.SemaphoreType.DMA((SIDE // UROWS,)),
+            pltpu.VMEM((SIDE, SIDE), jnp.float32), pltpu.SemaphoreType.DMA((SIDE // TILE,)),
         ],
         compiler_params=pltpu.CompilerParams(vmem_limit_bytes=UPDATE_LIMIT),
-        name="update",
+        name="finish",
     )(a, pr, pc_hi, pc_lo)
 
 
 def per_device(matrix):
-    return update(*panels(matrix))
+    return finish(*panels(matrix))
 
 
 def solution(mesh):

time: 53.1 us -> 43.7 us (0.82)
  the two profiles are of different devices: /device:TPU:128 before, /device:TPU:16 now
where the time goes in v3:
time: 43.7 us; the launch traced here: 43.6 us
  Pallas kernels  43.6 us (100%)
    pallas_call x1, Pallas kernels, panels(): pl.pallas_call(panels_kernel, out_shape=[pltpu.VMEM((SIDE, SIDE), f32), p...  39.4 us
    pallas_call x1, Pallas kernels, finish(): pl.pallas_call(finish_kernel, out_shape=jax.ShapeDtypeStruct((SIDE, SIDE)...  4.22 us

profile of v3, /device:TPU:16, one launch (start us, length us, event | category | flops | bytes accessed | tf_op | source)
XLA Modules:
  0.0 43.6 jit_solution(6467902255344354528)
XLA Ops:
  0.0 39.4 %panels.1 = (f32[1280,1280]{1,0:T(8,128)S(1)}, f32[1280,256]{1,0:T(8,128)S(1)}, bf16[256,1280]{1,0:T(8,128)(2,1)S(1)}, bf16[256,1280]{1,0:T(8,128)(2,1)S(1)}) custom-call(f32[1280,1280]{1,0:T(8,128)} %a_ref.1), custom_call_target="tpu_custom_call" | custom-call | tf_op jit(solution)/shard_map/panels/pallas_call | solution.py:516
  39.4 4.2 %finish.1 = f32[1280,1280]{1,0:T(8,128)} custom-call(f32[1280,1280]{1,0:T(8,128)S(1)} %get-tuple-element.9.a_ref, f32[1280,256]{1,0:T(8,128)S(1)} %get-tuple-element.10.pr_ref, bf16[256,1280]{1,0:T(8,128)(2,1)S(1)} %get-tuple-element.11.pc_hi_ref, bf16[256,1280]{1,0:T(8,128)(2,1)S(1)} %get-tuple-element.12.pc_lo_ref), custom_call_target="tpu_custom_call" | custom-call | tf_op jit(solution)/shard_map/finish/pallas_call | solution.py:580

commit v4 on v3

--- a/solution.py
+++ b/solution.py
@@ -17,11 +17,11 @@
 ZROWS = SIDE // ZCH
 PCH = 4
 PROWS = TILE // 4 // PCH
-FIRST = 11
+FIRST = 10
 CX = {4: (0,), 7: (1, 2)}
 CY = {8: (0,), 11: (1, 2)}
 PC_SLOT = 20
-PER_SLOT = 3
+PER_SLOT = 4
 VMEM_LIMIT = 40 * 2**20
 UPDATE_LIMIT = 24 * 2**20
 EXACT = lax.Precision.HIGHEST
@@ -116,6 +116,7 @@
 LEVEL = {(0, 0): 0, (1, 0): 1, (2, 0): 2, (1, 1): 2, (1, 3): 2, (2, 1): 3, (2, 3): 3, (1, 2): 3}
 STEPS = ((1, 0), (0, 1), (-1, 0), (0, -1))
 HOP = 3
+WAVE = 9
 Z_FAN = {0: (2, 6), 2: (1, 3, 4), 6: (5, 7)}
 
 
@@ -408,7 +409,7 @@
         if slot in CX:
             for tile in CX[slot]:
                 corner_x(tile)
-        if slot == 7:
+        if slot == WAVE:
             second_wave()
         if slot in CY:
             for tile in CY[slot]:
@@ -418,7 +419,7 @@
                 if HOP * level + j * 8 // ZCH == slot:
                     z_service(j, where_)
             for where_, level in ((7, 1), (6, 2)):
-                if 8 + HOP * level + j * 8 // ZCH == slot:
+                if WAVE + 1 + HOP * level + j * 8 // ZCH == slot:
                     z_service(j, where_)
         for j in range(PCH):
             for level in range(1, 4):
@@ -479,11 +480,15 @@
         yield
         while len(slots_seen) < 50:
             yield
+        for tile in range(3):
+            corner_drain(tile)
+        for index in range(8):
+            p_drain(index)
         rows_done()
 
     slots_seen = []
     steps = work()
-    for slot in range(1, 23):
+    for slot in range(1, WAVE + 16):
         slots_seen.append(slot)
         slot_work(slot)
         if slot >= FIRST:
@@ -493,8 +498,6 @@
     for _ in steps:
         pass
 
-    for tile in range(3):
-        corner_drain(tile)
     remote(whole_r, whole_r, z_sib_send, z_sib_recv.at[0], sibling).wait_send()
 
     @pl.when(jnp.logical_or(jnp.logical_or(pos == 1, pos == 2), jnp.logical_or(pos == 4, pos == 7)))
@@ -504,9 +507,6 @@
     @pl.when(jnp.logical_or(pos == 0, pos == 2))
     def _():
         z_sent(1)
-
-    for index in range(8):
-        p_drain(index)
 
 
 def panels(matrix):

time: 43.7 us -> 42.7 us (0.977)
  the two profiles are of different devices: /device:TPU:16 before, /device:TPU:113 now
where the time goes in v4:
time: 42.7 us; the launch traced here: 42.6 us
  Pallas kernels  42.5 us (100%)
    pallas_call x1, Pallas kernels, panels(): pl.pallas_call(panels_kernel, out_shape=[pltpu.VMEM((SIDE, SIDE), f32), p...  38.2 us
    pallas_call x1, Pallas kernels, finish(): pl.pallas_call(finish_kernel, out_shape=jax.ShapeDtypeStruct((SIDE, SIDE)...  4.22 us

profile of v4, /device:TPU:113, one launch (start us, length us, event | category | flops | bytes accessed | tf_op | source)
XLA Modules:
  0.0 42.6 jit_solution(4707917718726752862)
XLA Ops:
  0.0 38.2 %panels.1 = (f32[1280,1280]{1,0:T(8,128)S(1)}, f32[1280,256]{1,0:T(8,128)S(1)}, bf16[256,1280]{1,0:T(8,128)(2,1)S(1)}, bf16[256,1280]{1,0:T(8,128)(2,1)S(1)}) custom-call(f32[1280,1280]{1,0:T(8,128)} %a_ref.1), custom_call_target="tpu_custom_call" | custom-call | tf_op jit(solution)/shard_map/panels/pallas_call | solution.py:516
  38.3 4.2 %finish.1 = f32[1280,1280]{1,0:T(8,128)} custom-call(f32[1280,1280]{1,0:T(8,128)S(1)} %get-tuple-element.9.a_ref, f32[1280,256]{1,0:T(8,128)S(1)} %get-tuple-element.10.pr_ref, bf16[256,1280]{1,0:T(8,128)(2,1)S(1)} %get-tuple-element.11.pc_hi_ref, bf16[256,1280]{1,0:T(8,128)(2,1)S(1)} %get-tuple-element.12.pc_lo_ref), custom_call_target="tpu_custom_call" | custom-call | tf_op jit(solution)/shard_map/finish/pallas_call | solution.py:580

commit v5 on v4

--- a/solution.py
+++ b/solution.py
@@ -15,7 +15,7 @@
 RING_Z = 8
 ZCH = 16
 ZROWS = SIDE // ZCH
-PCH = 4
+PCH = 2
 PROWS = TILE // 4 // PCH
 FIRST = 10
 CX = {4: (0,), 7: (1, 2)}

time: 42.7 us -> 41.9 us (0.981)
  the two profiles are of different devices: /device:TPU:113 before, /device:TPU:215 now
where the time goes in v5:
time: 41.9 us; the launch traced here: 41.8 us
  Pallas kernels  41.8 us (100%)
    pallas_call x1, Pallas kernels, panels(): pl.pallas_call(panels_kernel, out_shape=[pltpu.VMEM((SIDE, SIDE), f32), p...  37.6 us
    pallas_call x1, Pallas kernels, finish(): pl.pallas_call(finish_kernel, out_shape=jax.ShapeDtypeStruct((SIDE, SIDE)...  4.22 us

profile of v5, /device:TPU:215, one launch (start us, length us, event | category | flops | bytes accessed | tf_op | source)
XLA Modules:
  0.0 41.8 jit_solution(920261990765014380)
XLA Ops:
  0.0 37.6 %panels.1 = (f32[1280,1280]{1,0:T(8,128)S(1)}, f32[1280,256]{1,0:T(8,128)S(1)}, bf16[256,1280]{1,0:T(8,128)(2,1)S(1)}, bf16[256,1280]{1,0:T(8,128)(2,1)S(1)}) custom-call(f32[1280,1280]{1,0:T(8,128)} %a_ref.1), custom_call_target="tpu_custom_call" | custom-call | tf_op jit(solution)/shard_map/panels/pallas_call | solution.py:516
  37.6 4.2 %finish.1 = f32[1280,1280]{1,0:T(8,128)} custom-call(f32[1280,1280]{1,0:T(8,128)S(1)} %get-tuple-element.9.a_ref, f32[1280,256]{1,0:T(8,128)S(1)} %get-tuple-element.10.pr_ref, bf16[256,1280]{1,0:T(8,128)(2,1)S(1)} %get-tuple-element.11.pc_hi_ref, bf16[256,1280]{1,0:T(8,128)(2,1)S(1)} %get-tuple-element.12.pc_lo_ref), custom_call_target="tpu_custom_call" | custom-call | tf_op jit(solution)/shard_map/finish/pallas_call | solution.py:580
